TPU v7x, 32 devices: a whole 2x2x4 slice. The times are simulated.
32 devices in a mesh: rx: 4 (over x, core), ry: 8 (over z, y).
Axes of the slice: x: 2, y: 2, z: 4, core: 2. Of those that a mesh axis runs over, the one named last changes fastest.
Arguments:
- panel: float32 [64, 524288], P(None, ('rx', 'ry')), may hold values from -6 to 6
- signs: int32 [524288], P(('rx', 'ry')), may hold values from -1 to 1, as said below
- sample_block: int32 [768], P(('rx', 'ry')), may hold values from 0 to 127
- sample_owner: int32 [768, 1], P(('rx', 'ry')), may hold values from 0 to 7; in each aligned block of 24 rows (0 to 23, 24 to 47, ...) at most 4 rows name the same one
Outputs:
- mixed: float32 [64, 524288], P(None, ('rx', 'ry'))
- sketch_blocks: float32 [64, 1024, 128], P(None, ('rx', 'ry'))
- r_factor: float32 [64, 64], replicated
- leverage: float32 [524288], P(('rx', 'ry'))
Inputs may be any that keep to these rules, and one draw needn't show every extreme that they name: `signs`: each entry is +1 or -1. `sample_owner`: among the 24 entries of one device no owner is named more than 4 times; in every draw some device names some owner exactly 4 times.
All inputs are finite; a program needn't handle non-finite values.
Results may differ from a plain program's by a relative error of at most 0.0003.
Values sent between devices are 32-bit elements; how exact they have to be, the bound alone decides.
A program may use at most 64 MiB of HBM per device.

v0:
```python
import math

import jax
import jax.numpy as jnp
from jax import lax
from jax.sharding import PartitionSpec as P

BLOCK = 128
K = 24
CAP = 4


PRECISE = lax.Precision.HIGHEST


def from_partner(value, axis, distance):
    mask = 2**distance
    pairs = [(source, source ^ mask) for source in range(lax.axis_size(axis))]
    return lax.ppermute(value, axis, pairs)


def hadamard(length):
    index_set = jnp.arange(length, dtype=jnp.int32)
    intersection = jnp.bitwise_and(index_set[:, None], index_set[None, :])
    parity = jnp.zeros((length, length), jnp.int32)
    for bit_index in range(max(length.bit_length() - 1, 1)):
        parity = parity + jnp.bitwise_and(jnp.right_shift(intersection, bit_index), 1)
    return (1.0 - 2.0 * jnp.bitwise_and(parity, 1)).astype(jnp.float32)


def triangle(matrix):
    col_count, row_count = matrix.shape
    index_set = jnp.arange(row_count, dtype=jnp.int32)

    def reflect(column_id, current):
        column = lax.dynamic_index_in_dim(current, column_id, 0, keepdims=False)
        below = jnp.where(index_set >= column_id, column, jnp.zeros_like(column))
        head_value = lax.dynamic_index_in_dim(column, column_id, 0, keepdims=False)
        col_norm = jnp.sqrt(jnp.sum(below * below))
        sign_value = jnp.where(head_value >= 0, 1.0, -1.0).astype(current.dtype)
        alpha_value = -sign_value * col_norm
        vector = below - alpha_value * (index_set == column_id).astype(current.dtype)
        beta_value = jnp.sum(vector * vector)
        safe_beta = jnp.where(beta_value > 0, beta_value, jnp.ones_like(beta_value))
        factor_coef = jnp.where(beta_value > 0, 2.0 / safe_beta, jnp.zeros_like(beta_value))
        projection = jnp.dot(current, vector, precision=PRECISE)
        return current - factor_coef * projection[:, None] * vector[None, :]

    reduced = lax.fori_loop(0, col_count, reflect, matrix)
    square = reduced[:, :col_count]
    col_ids = jnp.arange(col_count, dtype=jnp.int32)
    upper = jnp.where(col_ids[None, :] <= col_ids[:, None], square, jnp.zeros_like(square))
    diagonal = jnp.diagonal(upper)
    sign_flip = jnp.where(diagonal >= 0, 1.0, -1.0).astype(matrix.dtype)
    return upper * sign_flip[None, :]


def lower_inverse(lower):
    order = lower.shape[0]
    identity = jnp.eye(order, dtype=lower.dtype)

    def one_row(row_id, inverse):
        row_vals = lax.dynamic_index_in_dim(lower, row_id, 0, keepdims=False)
        unit_row = lax.dynamic_index_in_dim(identity, row_id, 0, keepdims=False)
        pivot = lax.dynamic_index_in_dim(row_vals, row_id, 0, keepdims=False)
        new_row = (unit_row - jnp.dot(row_vals, inverse, precision=PRECISE)) / pivot
        return lax.dynamic_update_index_in_dim(inverse, new_row, row_id, 0)

    return lax.fori_loop(0, order, one_row, jnp.zeros_like(lower))


def place_blocks(blocks, pick_ids, owner_ids, slot_count):
    picked = jnp.take(blocks, pick_ids, axis=1)
    order_ids = jnp.arange(owner_ids.shape[0], dtype=jnp.int32)
    earlier = jnp.logical_and(
        owner_ids[:, None] == owner_ids[None, :], order_ids[None, :] < order_ids[:, None]
    )
    rank_slot = jnp.sum(earlier.astype(jnp.int32), axis=1)
    slot_index = owner_ids * CAP + rank_slot
    one_hot = (jnp.arange(slot_count, dtype=jnp.int32)[:, None] == slot_index[None, :]).astype(
        blocks.dtype
    )
    return jnp.einsum("sk,ckb->csb", one_hot, picked, precision=PRECISE)


def per_device(panel, signs, sample_block, sample_owner):
    col_count, row_count = panel.shape
    block_rows = row_count // 128
    low_count = lax.axis_size("ry")
    high_count = lax.axis_size("rx")
    device_count = low_count * high_count
    signed = panel * signs.astype(jnp.float32)[None, :]
    blocked = signed.reshape(col_count, block_rows, 128)
    blocked = jnp.einsum("cab,bk->cak", blocked, hadamard(128), precision=PRECISE)
    blocked = jnp.einsum("cab,ak->ckb", blocked, hadamard(block_rows), precision=PRECISE)
    flattened = blocked.reshape(col_count, row_count) * (1.0 / math.sqrt(row_count * device_count))
    mixed = flattened
    for bit_index in range(low_count.bit_length() - 1):
        partner = from_partner(mixed, "ry", bit_index)
        own_bit = jnp.bitwise_and(jnp.right_shift(lax.axis_index("ry"), bit_index), 1)
        mixed = jnp.where(own_bit == 0, mixed + partner, partner - mixed)
    for bit_index in range(high_count.bit_length() - 1):
        partner = from_partner(mixed, "rx", bit_index)
        own_bit = jnp.bitwise_and(jnp.right_shift(lax.axis_index("rx"), bit_index), 1)
        mixed = jnp.where(own_bit == 0, mixed + partner, partner - mixed)
    slot_count = low_count * CAP
    blocks = mixed.reshape(col_count, row_count // BLOCK, BLOCK)
    outgoing = place_blocks(blocks, sample_block, sample_owner[:, 0], slot_count)
    received = lax.all_to_all(outgoing, "ry", split_axis=1, concat_axis=1, tiled=True)
    leaf_factor = triangle(received.reshape(col_count, slot_count * BLOCK))
    all_leaves = lax.all_gather(leaf_factor, ("rx", "ry"), axis=1, tiled=True)
    factor = triangle(all_leaves)
    sketch_rows = K * BLOCK * device_count
    r_factor = factor.T / math.sqrt(sketch_rows)
    inverse = lower_inverse(r_factor.T)
    solved = jnp.dot(inverse, panel, precision=PRECISE)
    leverage = jnp.sum(solved * solved, axis=0) / col_count
    return (mixed, received, r_factor, leverage)


def solution(mesh):
    in_specs = (P(None, ("rx", "ry")), P(("rx", "ry")), P(("rx", "ry")), P(("rx", "ry"), None))
    out_specs = (P(None, ("rx", "ry")), P(None, ("rx", "ry"), None), P(), P(("rx", "ry")))
    return jax.shard_map(
        per_device, mesh=mesh, in_specs=in_specs, out_specs=out_specs, check_vma=False
    )
```

profile of v0, /device:TPU:0, one launch (start us, length us, event | category | flops | bytes accessed | tf_op | source)
XLA Modules:
  0.0 1447.9 jit_solution(7102140658455049365)
XLA Ops:
  1.5 2.5 multiply_bitcast_fusion
  4.7 3.6 fusion.20
  8.4 4.0 convolution_multiply_fusion.1
  12.4 4.4 copy.73
  16.8 3.0 collective-permute-start
  19.7 90.9 %collective-permute-done = f32[64,16384]{1,0:T(8,128)} collective-permute-done((f32[64,16384]{1,0:T(8,128)}, f32[64,16384]{1,0:T(8,128)}, u32[]{:S(2)}, u32[]{:S(2)}) %collective-permute-start) | collective-permute-done | bytes 4194336 | tf_op jit(solution)/shard_map/ppermute | solution.py:19
  110.6 8.5 subtract_select_fusion.4
  119.1 1.8 collective-permute-start.1
  120.9 90.3 %collective-permute-done.1 = f32[64,16384]{1,0:T(8,128)} collective-permute-done((f32[64,16384]{1,0:T(8,128)}, f32[64,16384]{1,0:T(8,128)}, u32[]{:S(2)}, u32[]{:S(2)}) %collective-permute-start.1) | collective-permute-done | bytes 4194336 | tf_op jit(solution)/shard_map/ppermute | solution.py:19
  211.1 5.9 subtract_select_fusion.3
  217.1 2.5 collective-permute-start.2
  219.6 179.4 %collective-permute-done.2 = f32[64,16384]{1,0:T(8,128)} collective-permute-done((f32[64,16384]{1,0:T(8,128)}, f32[64,16384]{1,0:T(8,128)}, u32[]{:S(2)}, u32[]{:S(2)}) %collective-permute-start.2) | collective-permute-done | bytes 4194336 | tf_op jit(solution)/shard_map/ppermute | solution.py:19
  399.0 5.9 subtract_select_fusion.2
  404.9 7.5 collective-permute-done.3
  412.4 5.9 subtract_select_fusion.1
  418.3 1.1 collective-permute-start.4
  419.6 91.6 %collective-permute-done.4 = f32[64,16384]{1,0:T(8,128)} collective-permute-done((f32[64,16384]{1,0:T(8,128)}, f32[64,16384]{1,0:T(8,128)}, u32[]{:S(2)}, u32[]{:S(2)}) %collective-permute-start.4) | collective-permute-done | bytes 4194336 | tf_op jit(solution)/shard_map/ppermute | solution.py:19
  511.3 3.9 subtract_select_fusion
  515.2 2.0 copy-done.1
  517.2 2.5 copy_bitcast_fusion.1
  519.7 2.8 gather_fusion
  522.6 1.1 convolution_bitcast_fusion.3
  523.8 1.6 copy.51
  525.4 5.3 all-to-all-start
  530.7 25.4 %all-to-all-done = f32[64,32,128]{2,0,1:T(8,128)S(1)} async-done(((f32[64,32,128]{2,0,1:T(8,128)}), f32[64,32,128]{2,0,1:T(8,128)S(1)}, u32[]{:S(2)}, u32[]{:S(2)}) %all-to-all-start) | async-done | bytes 1048608 | tf_op jit(solution)/shard_map/all_to_all | solution.py:109
  556.2 378.5 %while.53 = (s32[]{:T(128)}, f32[64,4096]{1,0:T(8,128)S(1)}, s32[]{:T(128)}, s32[]{:T(128)}, s32[]{:T(128)}, /*index=5*/s32[]{:T(128)}, f32[1,1]{1,0:T(1,128)}, ...) while((s32[]{:T(128)}, f32[64,4096]{1,0:T(8,128)S(1)}, ...), condition=%wide.region_4.5_spmd.clone.clone, body=%wide.region_1.4_spmd.clone.clone.sunk | while | flops 3727434 | bytes 3334958 | solution.py:49
  934.7 2.0 copy.53
  939.1 72.5 %all_gather.3 = f32[64,2048]{0,1:T(8,128)S(1)} all-gather(f32[64,64]{0,1:T(8,128)S(1)} %broadcast_multiply_fusion.1), channel_id=1, replica_groups=mesh['rx'=4,'ry'=8] {'rx','ry'}, dimensions={1}, use_global_device_ids=true | all-gather | bytes 540672 | tf_op jit(solution)/shard_map/all_gather | solution.py:111
  1012.0 334.8 %while.54 = (s32[]{:T(128)}, f32[64,2048]{1,0:T(8,128)S(1)}, s32[]{:T(128)}, s32[]{:T(128)}, s32[]{:T(128)}, /*index=5*/s32[]{:T(128)}, f32[1,1]{1,0:T(1,128)}, ...) while((s32[]{:T(128)}, f32[64,2048]{1,0:T(8,128)S(1)}, ...), condition=%wide.region_8.9_spmd.clone.clone, body=%wide.region_5.8_spmd.clone.clone.sunk | while | flops 1863754 | bytes 1667886 | solution.py:49
  1348.8 90.5 %while.52 = (s32[]{:T(128)}, f32[64,64]{1,0:T(8,128)S(1)}, f32[64,64]{1,0:T(8,128)S(1)}, f32[64,64]{1,0:T(8,128)S(1)}, s32[]{:T(128)}, /*index=5*/s32[]{:T(128)}, s32[]{:T(128)}) while((s32[]{:T(128)}, f32[64,64]{1,0:T(8,128)S(1)}, f32[64,64]{1,0:T(8,128)S(1)}, f32[64,64]{1,0:T(8,128)S(1)}, s32[]{:T(128)}, /*index=5*/s32[]{:T(128)}, ...), condition=%wide.region_10.11_spmd, body=%wide.region_9.10_spmd.sunk | while | flops 49283 | bytes 35705 | solution.py:69
  1439.3 6.4 fusion.18
  1446.3 1.6 copy.58
  (1249 shorter events, 457.6 us)
Async XLA Ops:
  12.3 4.4 copy-start
  16.8 93.8 %collective-permute-start = (f32[64,16384]{1,0:T(8,128)}, f32[64,16384]{1,0:T(8,128)}, u32[]{:S(2)}, u32[]{:S(2)}) collective-permute-start(f32[64,16384]{1,0:T(8,128)} %bitcast.82), channel_id=1, source_target_pairs={{0,1},{1,0},{2,3},{3,2},{4,5},{5,4},{6,7},{7,6},{8,9},{9,8},{10,11... | collective-permute-start | bytes 12582920 | tf_op jit(solution)/shard_map/ppermute | solution.py:19
  119.1 92.1 %collective-permute-start.1 = (f32[64,16384]{1,0:T(8,128)}, f32[64,16384]{1,0:T(8,128)}, u32[]{:S(2)}, u32[]{:S(2)}) collective-permute-start(f32[64,16384]{1,0:T(8,128)} %subtract_select_fusion.4), channel_id=1, source_target_pairs={{0,2},{1,3},{2,0},{3,1},{4,6},{5,7},{6,4},{7,5},{8,10},{9,11},{10,... | collective-permute-start | bytes 12582920 | tf_op jit(solution)/shard_map/ppermute | solution.py:19
  217.1 181.9 %collective-permute-start.2 = (f32[64,16384]{1,0:T(8,128)}, f32[64,16384]{1,0:T(8,128)}, u32[]{:S(2)}, u32[]{:S(2)}) collective-permute-start(f32[64,16384]{1,0:T(8,128)} %subtract_select_fusion.3), channel_id=1, source_target_pairs={{0,4},{1,5},{2,6},{3,7},{4,0},{5,1},{6,2},{7,3},{8,12},{9,13},{10,... | collective-permute-start | bytes 12582920 | tf_op jit(solution)/shard_map/ppermute | solution.py:19
  404.9 7.5 collective-permute-start.3
  404.9 14.5 %copy-start.2 = (s32[24]{0:T(128)S(1)}, s32[24]{0:T(128)}, u32[]{:S(2)}) copy-start(s32[24]{0:T(128)} %param.12) | copy-start | bytes 292
  404.9 14.5 %copy-start.3 = (s32[24,1]{0,1:T(1,128)S(1)}, s32[24,1]{0,1:T(1,128)}, u32[]{:S(2)}) copy-start(s32[24,1]{0,1:T(1,128)} %param.13) | copy-start | bytes 292
  418.3 92.9 %collective-permute-start.4 = (f32[64,16384]{1,0:T(8,128)}, f32[64,16384]{1,0:T(8,128)}, u32[]{:S(2)}, u32[]{:S(2)}) collective-permute-start(f32[64,16384]{1,0:T(8,128)} %subtract_select_fusion.1), channel_id=1, source_target_pairs={{0,16},{8,24},{16,0},{24,8},{1,17},{9,25},{17,1},{25,9},{2,18},{10... | collective-permute-start | bytes 12582920 | tf_op jit(solution)/shard_map/ppermute | solution.py:19
  515.2 2.0 copy-start.1
  525.4 30.8 %all-to-all-start = ((f32[64,32,128]{2,0,1:T(8,128)}), f32[64,32,128]{2,0,1:T(8,128)S(1)}, u32[]{:S(2)}, u32[]{:S(2)}) async-start(f32[64,32,128]{2,0,1:T(8,128)} %copy.51), calls=%async_computation | async-start | bytes 2097152 | tf_op jit(solution)/shard_map/all_to_all | solution.py:109
where the time goes:
time: 1450 us
  waiting for transfers between devices  485 us (33%)
  loops' own time  354 us (24%)
  other arithmetic  229 us (16%)
  matrix products  156 us (11%)
  local copies, waits for them, and re-layouts  137 us (9%)
  blocking collectives  72.5 us (5%)
    ppermute x5, waiting for transfers between devices, from_partner(): return lax.ppermute(value, axis, pairs)  460 us
    another operation x2, loops' own time, triangle(): reduced = lax.fori_loop(0, col_count, reflect, matrix)  352 us
    dot_general x128, matrix products, reflect(): projection = jnp.dot(current, vector, precision=PRECISE)  91.1 us
    reduce_sum x128, other arithmetic, reflect(): col_norm = jnp.sqrt(jnp.sum(below * below))  82.5 us
    reduce_sum x128, other arithmetic, reflect(): beta_value = jnp.sum(vector * vector)  77.5 us
    dynamic_slice x128, local copies, waits for them, and re-layouts, reflect(): head_value = lax.dynamic_index_in_dim(column, column_id, 0, keepdims=False)  75.5 us
    all_gather x1, blocking collectives, per_device(): all_leaves = lax.all_gather(leaf_factor, ('rx', 'ry'), axis=1, tiled=True)  72.5 us
    dot_general x64, matrix products, one_row(): new_row = (unit_row - jnp.dot(row_vals, inverse, precision=PRECISE)) / pivot  50 us
  transfers between devices with their start and end apart: 6, of which 6 were waited for; matrix products, arithmetic and copies ran while one was open for 0% of the time, Pallas kernels for 0%

commit v1 on v0

v1 whole, which is shorter than its diff:
```python
import functools
import math

import jax
import jax.numpy as jnp
from jax import lax
from jax.experimental import pallas as pl
from jax.experimental.pallas import tpu as pltpu
from jax.sharding import PartitionSpec as P

BLOCK = 128
K = 24
CAP = 4
LANES = 128
SUB = 8
STRIP = 2048

PRECISE = lax.Precision.HIGHEST


def hadamard(length):
    index_set = jnp.arange(length, dtype=jnp.int32)
    intersection = jnp.bitwise_and(index_set[:, None], index_set[None, :])
    parity = jnp.zeros((length, length), jnp.int32)
    for bit_index in range(max(length.bit_length() - 1, 1)):
        parity = parity + jnp.bitwise_and(jnp.right_shift(intersection, bit_index), 1)
    return (1.0 - 2.0 * jnp.bitwise_and(parity, 1)).astype(jnp.float32)


def own_bit(axis, bit_index):
    return lax.rem(lax.axis_index(axis) // 2**bit_index, 2)


def partner_of(axis, bit_index):
    return lax.axis_index(axis) + 2**bit_index * (1 - 2 * own_bit(axis, bit_index))


def bits_of(sizes):
    return [
        (axis, bit)
        for axis in ("ry", "rx")
        for bit in reversed(range(sizes[axis].bit_length() - 1))
    ]


def exchange_order(sizes, chunks):
    bits = bits_of(sizes)
    half_ry = (sizes["ry"].bit_length() - 1) // 2
    far = [b for b in bits if b[0] == "ry" and b[1] >= half_ry]
    near = [b for b in bits if b[0] == "ry" and b[1] < half_ry]
    cross = [b for b in bits if b[0] == "rx" and b[1] > 0]
    core = [b for b in bits if b[0] == "rx" and b[1] == 0]
    orders = []
    for chunk in range(chunks):
        if chunk % 2 == 0:
            orders.append(far + near + cross + core)
        else:
            orders.append(near + cross + core + far[::-1])

    def uses(bit):
        if bit in core:
            return {"core": 0.15}
        if bit in cross:
            return {"x": 2.0 ** (bit[1] - 1)}
        if bit in near:
            return {"y": 2.0 ** bit[1]}
        if bit[1] == half_ry:
            return {"edge": 1.0}
        return {"edge": 1.0, "mid": 2.0 ** (bit[1] - half_ry)}

    free, ready, stage, events = {}, [0.0] * chunks, [0] * chunks, []
    pending = []
    for chunk in range(chunks):
        pending.append((0.0, chunk))
    while pending:
        pending.sort()
        _, chunk = pending.pop(0)
        bit = orders[chunk][stage[chunk]]
        done = ready[chunk]
        for name, cost in uses(bit).items():
            done = max(done, max(free.get(name, 0.0), ready[chunk]) + cost)
        for name, cost in uses(bit).items():
            free[name] = max(free.get(name, 0.0), ready[chunk]) + cost
        events.append((done, chunk, stage[chunk]))
        ready[chunk] = done
        stage[chunk] += 1
        if stage[chunk] < len(orders[chunk]):
            pending.append((done, chunk))
    events.sort()
    return orders, [(chunk, step) for _, chunk, step in events]


def exchange_kernel(sizes, from_ref, used_ref, x_ref, mixed_ref, sketch_ref, land, staged,
                    keep, send_sem, recv_sem, out_sem, in_sem):
    col_count, row_count = x_ref.shape
    chunks = col_count // SUB
    low_count = sizes["ry"]
    bits = bits_of(sizes)
    me = lax.axis_index("ry")
    orders, events = exchange_order(sizes, chunks)

    barrier = pltpu.get_barrier_semaphore()
    greeted = 0
    for bit in bits:
        if bit[0] == "rx":
            pl.semaphore_signal(barrier, inc=1, device_id={"rx": partner_of(*bit)},
                                device_id_type=pl.DeviceIdType.MESH)
            greeted += 1
    for shift in range(1, low_count):
        pl.semaphore_signal(barrier, inc=1, device_id={"ry": lax.rem(me + shift, low_count)},
                            device_id_type=pl.DeviceIdType.MESH)
        greeted += 1
    pl.semaphore_wait(barrier, greeted)

    signs = {b: (1 - 2 * own_bit(*b)).astype(jnp.float32) for b in bits}
    waits = []

    def columns(chunk):
        return pl.ds(chunk * SUB, SUB)

    def source(chunk, step):
        if step == 0:
            return x_ref.at[columns(chunk)]
        return land.at[bits.index(orders[chunk][step - 1]), columns(chunk)]

    def send(chunk, step):
        bit = orders[chunk][step]
        where = bits.index(bit)
        copy = pltpu.make_async_remote_copy(
            src_ref=source(chunk, step),
            dst_ref=land.at[where, columns(chunk)],
            send_sem=send_sem.at[where, chunk],
            recv_sem=recv_sem.at[where, chunk],
            device_id={bit[0]: partner_of(*bit)},
            device_id_type=pl.DeviceIdType.MESH,
        )
        copy.start()
        waits.append(copy)
        return copy

    flight = {}
    for chunk in range(chunks):
        flight[chunk] = send(chunk, 0)
    arrivals = []
    for chunk, step in events:
        flight[chunk].wait_recv()
        bit = orders[chunk][step]
        last = step == len(bits) - 1
        own, other = source(chunk, step), land.at[bits.index(bit), columns(chunk)]
        into = mixed_ref.at[columns(chunk)] if last else other
        sign = signs[bit]

        def add(strip, carry, own=own, other=other, into=into, sign=sign, last=last):
            lanes = pl.ds(pl.multiple_of(strip * STRIP, STRIP), STRIP)
            total = other[:, lanes] + sign * own[:, lanes]
            into[:, lanes] = total
            if last:
                for at in range(STRIP // BLOCK):
                    keep[strip * (STRIP // BLOCK) + at] = total[:, at * BLOCK : (at + 1) * BLOCK]
            return carry

        lax.fori_loop(0, row_count // STRIP, add, 0)
        if not last:
            flight[chunk] = send(chunk, step + 1)
            continue

        def place(slot, carry, chunk=chunk):
            staged[slot, columns(chunk), :] = keep[from_ref[slot]] * used_ref[slot]
            return carry

        lax.fori_loop(0, low_count * CAP, place, 0)
        own_slots = pl.ds(me * CAP, CAP)
        for shift in range(1, low_count):
            to = lax.rem(me + shift, low_count)
            copy = pltpu.make_async_remote_copy(
                src_ref=staged.at[pl.ds(to * CAP, CAP), columns(chunk)],
                dst_ref=sketch_ref.at[own_slots, columns(chunk)],
                send_sem=out_sem.at[shift - 1, chunk],
                recv_sem=in_sem.at[shift - 1, chunk],
                device_id={"ry": to},
                device_id_type=pl.DeviceIdType.MESH,
            )
            copy.start()
            arrivals.append(copy)
        sketch_ref[own_slots, columns(chunk), :] = staged[own_slots, columns(chunk), :]
    for copy in arrivals:
        copy.wait()
    for copy in waits:
        copy.wait_send()


def exchange(sizes, x, from_block, used):
    col_count, row_count = x.shape
    chunks = col_count // SUB
    slots = sizes["ry"] * CAP
    bit_count = len(bits_of(sizes))
    vmem = pl.BlockSpec(memory_space=pltpu.VMEM)
    smem = pl.BlockSpec(memory_space=pltpu.SMEM)
    return pl.pallas_call(
        functools.partial(exchange_kernel, sizes),
        out_shape=(
            jax.ShapeDtypeStruct((col_count, row_count), jnp.float32),
            jax.ShapeDtypeStruct((slots, col_count, BLOCK), jnp.float32),
        ),
        in_specs=[smem, smem, vmem],
        out_specs=(vmem, vmem),
        scratch_shapes=[
            pltpu.VMEM((bit_count, col_count, row_count), jnp.float32),
            pltpu.VMEM((slots, col_count, BLOCK), jnp.float32),
            pltpu.VMEM((row_count // BLOCK, SUB, BLOCK), jnp.float32),
            pltpu.SemaphoreType.DMA((bit_count, chunks)),
            pltpu.SemaphoreType.DMA((bit_count, chunks)),
            pltpu.SemaphoreType.DMA((sizes["ry"] - 1, chunks)),
            pltpu.SemaphoreType.DMA((sizes["ry"] - 1, chunks)),
        ],
        compiler_params=pltpu.CompilerParams(
            collective_id=0, has_side_effects=True, vmem_limit_bytes=50 * 2**20
        ),
        name="exchange",
    )(from_block, used, x)


def reduce_columns(work):
    tiles, col_count, _ = work.shape
    lane = lax.broadcasted_iota(jnp.int32, (1, LANES), 1)
    for low in range(0, col_count, SUB):
        rest = slice(low, col_count)

        def reflect(column, carry, low=low, rest=rest):
            at = pl.ds(column, 1)
            here = lane == column
            below = jnp.where(lane >= column, work[0, at, :], 0.0)
            top = work[0, rest, :]
            square = below * below
            product = top * below
            for tile in range(1, tiles):
                vector = work[tile, at, :]
                square = square + vector * vector
                product = product + work[tile, rest, :] * vector
            norm2 = jnp.sum(square, axis=1, keepdims=True)
            head = jnp.sum(jnp.where(here, below, 0.0), axis=1, keepdims=True)
            across = jnp.sum(jnp.where(here, top, 0.0), axis=1, keepdims=True)
            product = jnp.sum(product, axis=1, keepdims=True)
            norm = jnp.sqrt(norm2)
            alpha = jnp.where(head >= 0, -norm, norm)
            half = norm2 + jnp.abs(head) * norm
            coef = jnp.where(half > 0, 1.0 / jnp.where(half > 0, half, 1.0), 0.0)
            project = coef * (product - alpha * across)
            first = below - jnp.where(here, alpha, 0.0)
            vectors = [first] + [work[tile, at, :] for tile in range(1, tiles)]
            for tile in range(tiles):
                work[tile, rest, :] = work[tile, rest, :] - project * vectors[tile]
            return carry

        lax.fori_loop(low, low + SUB, reflect, 0)
    square = work[0]
    row_id = lax.broadcasted_iota(jnp.int32, (col_count, LANES), 0)
    lane_id = lax.broadcasted_iota(jnp.int32, (col_count, LANES), 1)
    upper = jnp.where(lane_id <= row_id, square, 0.0)
    diagonal = jnp.sum(jnp.where(lane_id == row_id, upper, 0.0), axis=0, keepdims=True)
    return upper * jnp.where(diagonal >= 0, 1.0, -1.0)


def leaf_kernel(sketch_ref, leaf_ref, work):
    work[...] = sketch_ref[...]
    factor = reduce_columns(work)
    half = factor.shape[0] // 2
    lane = lax.broadcasted_iota(jnp.int32, (half, LANES), 1)
    leaf_ref[...] = jnp.where(lane < LANES // 2, factor[:half], pltpu.roll(factor[half:], LANES // 2, 1))


def leaf(sketch):
    _, col_count, _ = sketch.shape
    return pl.pallas_call(
        leaf_kernel,
        out_shape=jax.ShapeDtypeStruct((col_count // 2, LANES), jnp.float32),
        in_specs=[pl.BlockSpec(memory_space=pltpu.VMEM)],
        out_specs=pl.BlockSpec(memory_space=pltpu.VMEM),
        scratch_shapes=[pltpu.VMEM(sketch.shape, jnp.float32)],
        compiler_params=pltpu.CompilerParams(vmem_limit_bytes=16 * 2**20),
        name="leaf",
    )(sketch)


def gather_kernel(sizes, leaf_ref, all_ref, send_sem, recv_sem):
    bits = bits_of(sizes)
    barrier = pltpu.get_barrier_semaphore()
    for bit in bits:
        pl.semaphore_signal(barrier, inc=1, device_id={bit[0]: partner_of(*bit)},
                            device_id_type=pl.DeviceIdType.MESH)
    pl.semaphore_wait(barrier, len(bits))
    place = 0
    for level, bit in enumerate(bits):
        place = place + 2**level * own_bit(*bit)
    all_ref[pl.ds(place, 1)] = leaf_ref[...][None]
    for level, bit in enumerate(bits):
        width = 2**level
        held = all_ref.at[pl.ds(place // width * width, width)]
        copy = pltpu.make_async_remote_copy(
            src_ref=held, dst_ref=held,
            send_sem=send_sem.at[level], recv_sem=recv_sem.at[level],
            device_id={bit[0]: partner_of(*bit)}, device_id_type=pl.DeviceIdType.MESH,
        )
        copy.start()
        copy.wait()


def gather(sizes, leaf_factor):
    bit_count = len(bits_of(sizes))
    return pl.pallas_call(
        functools.partial(gather_kernel, sizes),
        out_shape=jax.ShapeDtypeStruct((sizes["rx"] * sizes["ry"],) + leaf_factor.shape, jnp.float32),
        in_specs=[pl.BlockSpec(memory_space=pltpu.VMEM)],
        out_specs=pl.BlockSpec(memory_space=pltpu.VMEM),
        scratch_shapes=[pltpu.SemaphoreType.DMA((bit_count,)), pltpu.SemaphoreType.DMA((bit_count,))],
        compiler_params=pltpu.CompilerParams(collective_id=1, has_side_effects=True),
        name="gather",
    )(leaf_factor)


def final_kernel(scale, all_ref, lower_ref, inverse_ref, work):
    leaves, half, _ = all_ref.shape
    col_count = 2 * half
    lane = lax.broadcasted_iota(jnp.int32, (half, LANES), 1)
    left = lane < LANES // 2
    for tile in range(leaves // 2):
        one, two = all_ref[2 * tile], all_ref[2 * tile + 1]
        work[tile, :half, :] = jnp.where(left, one, pltpu.roll(two, LANES // 2, 1))
        work[tile, half:, :] = jnp.where(left, pltpu.roll(one, LANES // 2, 1), two)
    lower = reduce_columns(work) / scale
    lower_ref[...] = lower
    row_id = lax.broadcasted_iota(jnp.int32, (SUB, LANES), 0)
    lane_id = lax.broadcasted_iota(jnp.int32, (SUB, LANES), 1)
    parts = [
        jnp.where(lane_id == row_id + SUB * part, 1.0, 0.0) for part in range(col_count // SUB)
    ]
    for row in range(col_count):
        part, at = divmod(row, SUB)
        solved = parts[part][at : at + 1, :] / lower[row : row + 1, row : row + 1]
        for later in range(part, col_count // SUB):
            factor = lower[later * SUB : (later + 1) * SUB, row : row + 1]
            reduced = parts[later] - factor * solved
            if later == part:
                reduced = jnp.where(
                    row_id == at, solved, jnp.where(row_id > at, reduced, parts[later])
                )
            parts[later] = reduced
    for part in range(col_count // SUB):
        inverse_ref[part * SUB : (part + 1) * SUB, :] = parts[part]


def final(all_leaves, scale):
    leaves, half, _ = all_leaves.shape
    col_count = 2 * half
    shape = jax.ShapeDtypeStruct((col_count, LANES), jnp.float32)
    vmem = pl.BlockSpec(memory_space=pltpu.VMEM)
    return pl.pallas_call(
        functools.partial(final_kernel, scale),
        out_shape=(shape, shape),
        in_specs=[vmem],
        out_specs=(vmem, vmem),
        scratch_shapes=[pltpu.VMEM((leaves // 2, col_count, LANES), jnp.float32)],
        compiler_params=pltpu.CompilerParams(vmem_limit_bytes=16 * 2**20),
        name="final",
    )(all_leaves)


def slot_sources(pick_ids, owner_ids, slot_count):
    order_ids = jnp.arange(owner_ids.shape[0], dtype=jnp.int32)
    earlier = jnp.logical_and(
        owner_ids[:, None] == owner_ids[None, :], order_ids[None, :] < order_ids[:, None]
    )
    rank_slot = jnp.sum(earlier.astype(jnp.int32), axis=1)
    slot_index = owner_ids * CAP + rank_slot
    match = (jnp.arange(slot_count, dtype=jnp.int32)[:, None] == slot_index[None, :]).astype(jnp.int32)
    return jnp.sum(match * pick_ids[None, :], axis=1), jnp.sum(match, axis=1).astype(jnp.float32)


def per_device(sizes, panel, signs, sample_block, sample_owner):
    col_count, row_count = panel.shape
    block_rows = row_count // LANES
    device_count = sizes["ry"] * sizes["rx"]
    from_block, used = slot_sources(sample_block, sample_owner[:, 0], sizes["ry"] * CAP)
    signed = panel * signs.astype(jnp.float32)[None, :]
    blocked = signed.reshape(col_count, block_rows, LANES)
    blocked = jnp.einsum("cab,bk->cak", blocked, hadamard(LANES), precision=PRECISE)
    blocked = jnp.einsum("cab,ak->ckb", blocked, hadamard(block_rows), precision=PRECISE)
    local = blocked.reshape(col_count, row_count) * (1.0 / math.sqrt(row_count * device_count))
    mixed, sketch = exchange(sizes, local, from_block, used)
    received = jnp.transpose(sketch, (1, 0, 2))
    all_leaves = gather(sizes, leaf(sketch))
    lower, inverse = final(all_leaves, math.sqrt(K * BLOCK * device_count))
    r_factor = lower[:, :col_count].T
    solved = jnp.dot(inverse[:, :col_count], panel, precision=PRECISE)
    leverage = jnp.sum(solved * solved, axis=0) / col_count
    return (mixed, received, r_factor, leverage)


def solution(mesh):
    sizes = {name: int(mesh.shape[name]) for name in ("rx", "ry")}
    in_specs = (P(None, ("rx", "ry")), P(("rx", "ry")), P(("rx", "ry")), P(("rx", "ry"), None))
    out_specs = (P(None, ("rx", "ry")), P(None, ("rx", "ry"), None), P(), P(("rx", "ry")))
    return jax.shard_map(
        functools.partial(per_device, sizes), mesh=mesh, in_specs=in_specs, out_specs=out_specs,
        check_vma=False,
    )
```

time: 1450 us -> 339 us (0.23)
  waiting for transfers between devices: 485 us -> 0 us
  loops' own time: 354 us -> 0 us
  Pallas kernels: 0 us -> 306 us
  other arithmetic: 229 us -> 6.31 us
  matrix products: 156 us -> 14.1 us
  local copies, waits for them, and re-layouts: 137 us -> 11.1 us
  blocking collectives: 72.5 us -> 0 us
    ppermute x5 -> x0, waiting for transfers between devices: 460 us -> none  [from_partner(): return lax.ppermute(value, axis, pairs)]
    another operation x3 -> x0, loops' own time: 354 us -> none  [the longest x2 352 us: triangle(): reduced = lax.fori_loop(0, col_count, reflect, matrix)]
    pallas_call x0 -> x4, Pallas kernels: none -> 306 us  [the longest x1 258 us: exchange(): pl.pallas_call(functools.partial(exchange_kernel, sizes), out_shape=(jax....]
    reduce_sum x257 -> x2, other arithmetic: 160 us -> 1.65 us  [the longest x1 0.91 us: slot_sources(): rank_slot = jnp.sum(earlier.astype(jnp.int32), axis=1)]
    dot_general x195 -> x2, matrix products: 152 us -> 10.1 us  [the longest x1 6.5 us: per_device(): solved = jnp.dot(inverse[:, :col_count], panel, precision=PRECISE)]
    dynamic_slice x320 -> x0, local copies, waits for them, and re-layouts: 116 us -> none  [the longest x128 75.5 us: reflect(): head_value = lax.dynamic_index_in_dim(column, column_id, 0, keepdims=False)]
    all_gather x1 -> x0, blocking collectives: 72.5 us -> none  [per_device(): all_leaves = lax.all_gather(leaf_factor, ('rx', 'ry'), axis=1, tiled=True)]
    sub x256 -> x0, other arithmetic: 31.1 us -> none  [the longest x128 27.6 us: reflect(): return current - factor_coef * projection[:, None] * vector[None, :]]
  transfers between devices with their start and end apart: 6 -> 0, of which waited for: 6 -> 0; matrix products, arithmetic and copies ran while one was open for 0% -> 0% of each run, Pallas kernels for 0% -> 0%
where the time goes in v1:
time: 339 us; the launch traced here: 338 us
  Pallas kernels  306 us (90%)
  matrix products  14.1 us (4%)
  local copies, waits for them, and re-layouts  11.1 us (3%)
  other arithmetic  6.31 us (2%)
    pallas_call x1, Pallas kernels, exchange(): pl.pallas_call(functools.partial(exchange_kernel, sizes), out_shape=(jax....  258 us
    pallas_call x1, Pallas kernels, gather(): pl.pallas_call(functools.partial(gather_kernel, sizes), out_shape=jax.Sha...  22.2 us
    pallas_call x1, Pallas kernels, leaf(): pl.pallas_call(leaf_kernel, out_shape=jax.ShapeDtypeStruct((col_count //...  15.7 us
    unnamed x11, local copies, waits for them, and re-layouts  11.1 us
    pallas_call x1, Pallas kernels, final(): pl.pallas_call(functools.partial(final_kernel, scale), out_shape=(shape,...  10.8 us

profile of v1, /device:TPU:0, one launch (start us, length us, event | category | flops | bytes accessed | tf_op | source)
XLA Modules:
  0.0 338.5 jit_solution(17860513694208604965)
XLA Ops:
  0.6 0.9 convert_reduce_fusion.1
  1.5 0.7 multiply_add_fusion
  2.2 0.7 convert_reduce_fusion
  3.0 0.8 convert_element_type.22
  3.8 2.5 multiply_bitcast_fusion
  6.3 0.7 copy.12
  7.1 3.6 %fusion.2 = f32[64,128,128]{2,1,0:T(8,128)S(1)} fusion(f32[64,128,128]{2,1,0:T(8,128)S(1)} %bitcast.23), kind=kOutput, calls=%fused_computation.6 | convolution fusion | flops 1611022336 | bytes 8388608 | tf_op jit(solution)/shard_map/cab,bk->cak/dot_general | solution.py:386
  10.7 4.0 %convolution_multiply_fusion.1 = f32[128,64,128]{2,0,1:T(8,128)S(1)} fusion(f32[64,128,128]{2,1,0:T(8,128)S(1)} %fusion.2), kind=kOutput, calls=%fused_computation.3 | convolution fusion | flops 1612070912 | bytes 8388608 | tf_op jit(solution)/shard_map/cab,ak->ckb/dot_general | solution.py:387
  14.7 4.4 %copy.15 = f32[8,8,128,128]{3,1,2,0:T(8,128)} copy(f32[8,8,128,128]{3,2,1,0:T(8,128)S(1)} %bitcast.24) | data formatting | bytes 8388608
  19.1 257.6 %exchange.1 = (f32[64,16384]{1,0:T(8,128)}, f32[32,64,128]{2,1,0:T(8,128)S(1)}) custom-call(s32[32]{0:T(128)S(1)} %get-tuple-element.21.from_ref, f32[32]{0:T(128)S(1)} %convert_element_type.20.used_ref, f32[64,16384]{1,0:T(8,128)} %bitcast.22), custom_call_target="tpu_custom_call" | custom-call | tf_op jit(solution)/shard_map/exchange/pallas_call | solution.py:199
  276.7 15.7 %leaf.1.leaf_ref = f32[32,128]{1,0:T(8,128)S(1)} custom-call(f32[32,64,128]{2,1,0:T(8,128)S(1)} %get-tuple-element.9.sketch_ref), custom_call_target="tpu_custom_call" | custom-call | tf_op jit(solution)/shard_map/leaf/pallas_call | solution.py:274
  292.4 0.0 copy-start.1
  292.4 0.6 copy-done.1
  293.0 22.2 %gather.1.all_ref = f32[32,32,128]{2,1,0:T(8,128)} custom-call(f32[32,128]{1,0:T(8,128)} %copy-done.1), custom_call_target="tpu_custom_call" | custom-call | tf_op jit(solution)/shard_map/gather/pallas_call | solution.py:310
  315.1 0.0 copy-start
  315.2 1.0 copy-done
  316.2 10.8 %final.1 = (f32[64,128]{1,0:T(8,128)S(1)}, f32[64,128]{1,0:T(8,128)S(1)}) custom-call(f32[32,32,128]{2,1,0:T(8,128)S(1)} %copy-done), custom_call_target="tpu_custom_call" | custom-call | tf_op jit(solution)/shard_map/final/pallas_call | solution.py:357
  327.0 0.7 copy.11
  327.7 0.0 copy-start.2
  327.7 6.5 %fusion = f32[16384]{0:T(1024)S(1)} fusion(f32[64,16384]{1,0:T(8,128)} %param.4, f32[64,128]{1,0:T(8,128)S(1)} %get-tuple-element.11), kind=kOutput, calls=%fused_computation.4 | convolution fusion | flops 807387136 | bytes 4292608 | tf_op jit(solution)/shard_map/dot_general | solution.py:394
  334.2 0.6 broadcast_multiply_fusion
  334.9 1.6 copy.10
  336.5 0.0 copy-done.2
  336.5 2.0 copy.17
  (2 shorter events, 0.0 us)
Async XLA Ops:
  292.4 0.6 copy-start.1
  315.1 1.0 copy-start
  327.7 8.7 %copy-start.2 = (f32[64,16384]{1,0:T(8,128)S(1)}, f32[64,16384]{1,0:T(8,128)}, u32[]{:S(2)}) copy-start(f32[64,16384]{1,0:T(8,128)} %get-tuple-element.26) | copy-start | bytes 12582916

commit v2 on v1

--- a/solution.py
+++ b/solution.py
@@ -14,6 +14,8 @@
 LANES = 128
 SUB = 8
 STRIP = 2048
+PARTS = 2
+DEPTH = 2
 
 PRECISE = lax.Precision.HIGHEST
 
@@ -43,7 +45,7 @@
     ]
 
 
-def exchange_order(sizes, chunks):
+def exchange_plan(sizes, units):
     bits = bits_of(sizes)
     half_ry = (sizes["ry"].bit_length() - 1) // 2
     far = [b for b in bits if b[0] == "ry" and b[1] >= half_ry]
@@ -51,11 +53,10 @@
     cross = [b for b in bits if b[0] == "rx" and b[1] > 0]
     core = [b for b in bits if b[0] == "rx" and b[1] == 0]
     orders = []
-    for chunk in range(chunks):
-        if chunk % 2 == 0:
-            orders.append(far + near + cross + core)
-        else:
-            orders.append(near + cross + core + far[::-1])
+    for unit in range(units):
+        deep = far if unit % 2 == 0 else far[::-1]
+        rest = near + cross + core if unit // 2 % 2 == 0 else cross + core + near
+        orders.append(deep + rest if unit < units // 2 else rest + deep)
 
     def uses(bit):
         if bit in core:
@@ -68,26 +69,41 @@
             return {"edge": 1.0}
         return {"edge": 1.0, "mid": 2.0 ** (bit[1] - half_ry)}
 
-    free, ready, stage, events = {}, [0.0] * chunks, [0] * chunks, []
-    pending = []
-    for chunk in range(chunks):
-        pending.append((0.0, chunk))
-    while pending:
-        pending.sort()
-        _, chunk = pending.pop(0)
-        bit = orders[chunk][stage[chunk]]
-        done = ready[chunk]
-        for name, cost in uses(bit).items():
-            done = max(done, max(free.get(name, 0.0), ready[chunk]) + cost)
-        for name, cost in uses(bit).items():
-            free[name] = max(free.get(name, 0.0), ready[chunk]) + cost
-        events.append((done, chunk, stage[chunk]))
-        ready[chunk] = done
-        stage[chunk] += 1
-        if stage[chunk] < len(orders[chunk]):
-            pending.append((done, chunk))
-    events.sort()
-    return orders, [(chunk, step) for _, chunk, step in events]
+    active, steps = {}, []
+    waiting = {bit: [(unit, 0) for unit in range(units) if orders[unit][0] == bit] for bit in bits}
+    counts = {bit: 0 for bit in bits}
+
+    def admit(bit):
+        waiting[bit].sort()
+        while waiting[bit] and counts[bit] < DEPTH:
+            unit, step = waiting[bit].pop(0)
+            counts[bit] += 1
+            active[(unit, step)] = 1.0
+            steps.append(("start", unit, step))
+
+    for bit in bits:
+        admit(bit)
+    while active:
+        load = {}
+        for unit, step in active:
+            for name, cost in uses(orders[unit][step]).items():
+                load[name] = load.get(name, 0.0) + cost
+        rates = {
+            key: 1.0 / max(load[name] for name in uses(orders[key[0]][key[1]])) for key in active
+        }
+        span, unit, step = min((active[key] / rates[key],) + key for key in active)
+        for key in active:
+            active[key] -= span * rates[key]
+        del active[(unit, step)]
+        bit = orders[unit][step]
+        counts[bit] -= 1
+        steps.append(("take", unit, step))
+        admit(bit)
+        steps.append(("add", unit, step))
+        if step + 1 < len(bits):
+            waiting[orders[unit][step + 1]].append((unit, step + 1))
+            admit(orders[unit][step + 1])
+    return orders, steps
 
 
 def exchange_kernel(sizes, from_ref, used_ref, x_ref, mixed_ref, sketch_ref, land, staged,
@@ -97,7 +113,9 @@
     low_count = sizes["ry"]
     bits = bits_of(sizes)
     me = lax.axis_index("ry")
-    orders, events = exchange_order(sizes, chunks)
+    units = chunks * PARTS
+    part = row_count // PARTS
+    orders, steps = exchange_plan(sizes, units)
 
     barrier = pltpu.get_barrier_semaphore()
     greeted = 0
@@ -118,54 +136,61 @@
     def columns(chunk):
         return pl.ds(chunk * SUB, SUB)
 
-    def source(chunk, step):
+    def piece(unit):
+        return columns(unit // PARTS), pl.ds(unit % PARTS * part, part)
+
+    def source(unit, step):
         if step == 0:
-            return x_ref.at[columns(chunk)]
-        return land.at[bits.index(orders[chunk][step - 1]), columns(chunk)]
-
-    def send(chunk, step):
-        bit = orders[chunk][step]
+            return x_ref.at[piece(unit)]
+        return land.at[(bits.index(orders[unit][step - 1]),) + piece(unit)]
+
+    flight, arrivals, done = {}, [], [0] * chunks
+    for kind, unit, step in steps:
+        bit = orders[unit][step]
         where = bits.index(bit)
-        copy = pltpu.make_async_remote_copy(
-            src_ref=source(chunk, step),
-            dst_ref=land.at[where, columns(chunk)],
-            send_sem=send_sem.at[where, chunk],
-            recv_sem=recv_sem.at[where, chunk],
-            device_id={bit[0]: partner_of(*bit)},
-            device_id_type=pl.DeviceIdType.MESH,
-        )
-        copy.start()
-        waits.append(copy)
-        return copy
-
-    flight = {}
-    for chunk in range(chunks):
-        flight[chunk] = send(chunk, 0)
-    arrivals = []
-    for chunk, step in events:
-        flight[chunk].wait_recv()
-        bit = orders[chunk][step]
+        own, other = source(unit, step), land.at[(where,) + piece(unit)]
+        if kind == "start":
+            copy = pltpu.make_async_remote_copy(
+                src_ref=own,
+                dst_ref=other,
+                send_sem=send_sem.at[where, unit],
+                recv_sem=recv_sem.at[where, unit],
+                device_id={bit[0]: partner_of(*bit)},
+                device_id_type=pl.DeviceIdType.MESH,
+            )
+            copy.start()
+            waits.append(copy)
+            flight[unit] = copy
+            continue
+        if kind == "take":
+            flight[unit].wait_recv()
+            continue
+        chunk = unit // PARTS
         last = step == len(bits) - 1
-        own, other = source(chunk, step), land.at[bits.index(bit), columns(chunk)]
-        into = mixed_ref.at[columns(chunk)] if last else other
+        into = mixed_ref.at[piece(unit)] if last else other
+        first = unit % PARTS * part // BLOCK
         sign = signs[bit]
 
-        def add(strip, carry, own=own, other=other, into=into, sign=sign, last=last):
+        def add(strip, carry, own=own, other=other, into=into, sign=sign, last=last, first=first):
             lanes = pl.ds(pl.multiple_of(strip * STRIP, STRIP), STRIP)
             total = other[:, lanes] + sign * own[:, lanes]
             into[:, lanes] = total
             if last:
                 for at in range(STRIP // BLOCK):
-                    keep[strip * (STRIP // BLOCK) + at] = total[:, at * BLOCK : (at + 1) * BLOCK]
+                    block = total[:, at * BLOCK : (at + 1) * BLOCK]
+                    keep[chunk_slot, first + strip * (STRIP // BLOCK) + at] = block
             return carry
 
-        lax.fori_loop(0, row_count // STRIP, add, 0)
+        chunk_slot = chunk
+        lax.fori_loop(0, part // STRIP, add, 0)
         if not last:
-            flight[chunk] = send(chunk, step + 1)
             continue
+        done[chunk] += 1
+        if done[chunk] < PARTS:
+            continue
 
         def place(slot, carry, chunk=chunk):
-            staged[slot, columns(chunk), :] = keep[from_ref[slot]] * used_ref[slot]
+            staged[slot, columns(chunk), :] = keep[chunk, from_ref[slot]] * used_ref[slot]
             return carry
 
         lax.fori_loop(0, low_count * CAP, place, 0)
@@ -207,9 +232,9 @@
         scratch_shapes=[
             pltpu.VMEM((bit_count, col_count, row_count), jnp.float32),
             pltpu.VMEM((slots, col_count, BLOCK), jnp.float32),
-            pltpu.VMEM((row_count // BLOCK, SUB, BLOCK), jnp.float32),
-            pltpu.SemaphoreType.DMA((bit_count, chunks)),
-            pltpu.SemaphoreType.DMA((bit_count, chunks)),
+            pltpu.VMEM((chunks, row_count // BLOCK, SUB, BLOCK), jnp.float32),
+            pltpu.SemaphoreType.DMA((bit_count, chunks * PARTS)),
+            pltpu.SemaphoreType.DMA((bit_count, chunks * PARTS)),
             pltpu.SemaphoreType.DMA((sizes["ry"] - 1, chunks)),
             pltpu.SemaphoreType.DMA((sizes["ry"] - 1, chunks)),
         ],
@@ -282,24 +307,42 @@
     )(sketch)
 
 
-def gather_kernel(sizes, leaf_ref, all_ref, send_sem, recv_sem):
-    bits = bits_of(sizes)
+def gather_kernel(sizes, leaf_ref, all_ref, send_sem, recv_sem, near_send, near_recv):
+    low_count = sizes["ry"]
+    bits = [bit for bit in bits_of(sizes) if bit[0] == "rx"]
+    me = lax.axis_index("ry")
     barrier = pltpu.get_barrier_semaphore()
     for bit in bits:
-        pl.semaphore_signal(barrier, inc=1, device_id={bit[0]: partner_of(*bit)},
+        pl.semaphore_signal(barrier, inc=1, device_id={"rx": partner_of(*bit)},
                             device_id_type=pl.DeviceIdType.MESH)
-    pl.semaphore_wait(barrier, len(bits))
-    place = 0
+    for shift in range(1, low_count):
+        pl.semaphore_signal(barrier, inc=1, device_id={"ry": lax.rem(me + shift, low_count)},
+                            device_id_type=pl.DeviceIdType.MESH)
+    pl.semaphore_wait(barrier, len(bits) + low_count - 1)
+    group = 0
     for level, bit in enumerate(bits):
-        place = place + 2**level * own_bit(*bit)
-    all_ref[pl.ds(place, 1)] = leaf_ref[...][None]
+        group = group + 2**level * own_bit(*bit)
+    place = pl.ds(group * low_count + me, 1)
+    all_ref[place] = leaf_ref[...][None]
+    copies = []
+    for shift in range(1, low_count):
+        copy = pltpu.make_async_remote_copy(
+            src_ref=all_ref.at[place], dst_ref=all_ref.at[place],
+            send_sem=near_send.at[shift - 1], recv_sem=near_recv.at[shift - 1],
+            device_id={"ry": lax.rem(me + shift, low_count)},
+            device_id_type=pl.DeviceIdType.MESH,
+        )
+        copy.start()
+        copies.append(copy)
+    for copy in copies:
+        copy.wait()
     for level, bit in enumerate(bits):
         width = 2**level
-        held = all_ref.at[pl.ds(place // width * width, width)]
+        held = all_ref.at[pl.ds(group // width * width * low_count, width * low_count)]
         copy = pltpu.make_async_remote_copy(
             src_ref=held, dst_ref=held,
             send_sem=send_sem.at[level], recv_sem=recv_sem.at[level],
-            device_id={bit[0]: partner_of(*bit)}, device_id_type=pl.DeviceIdType.MESH,
+            device_id={"rx": partner_of(*bit)}, device_id_type=pl.DeviceIdType.MESH,
         )
         copy.start()
         copy.wait()
@@ -312,7 +355,12 @@
         out_shape=jax.ShapeDtypeStruct((sizes["rx"] * sizes["ry"],) + leaf_factor.shape, jnp.float32),
         in_specs=[pl.BlockSpec(memory_space=pltpu.VMEM)],
         out_specs=pl.BlockSpec(memory_space=pltpu.VMEM),
-        scratch_shapes=[pltpu.SemaphoreType.DMA((bit_count,)), pltpu.SemaphoreType.DMA((bit_count,))],
+        scratch_shapes=[
+            pltpu.SemaphoreType.DMA((bit_count,)),
+            pltpu.SemaphoreType.DMA((bit_count,)),
+            pltpu.SemaphoreType.DMA((sizes["ry"] - 1,)),
+            pltpu.SemaphoreType.DMA((sizes["ry"] - 1,)),
+        ],
         compiler_params=pltpu.CompilerParams(collective_id=1, has_side_effects=True),
         name="gather",
     )(leaf_factor)

time: 339 us -> 293 us (0.86)
  Pallas kernels: 306 us -> 261 us
    pallas_call x1, Pallas kernels: 258 us -> 221 us  [exchange(): pl.pallas_call(functools.partial(exchange_kernel, sizes), out_shape=(jax....]
    pallas_call x1, Pallas kernels: 22.2 us -> 13.2 us  [gather(): pl.pallas_call(functools.partial(gather_kernel, sizes), out_shape=jax.Sha...]
where the time goes in v2:
time: 293 us
  Pallas kernels  261 us (89%)
  matrix products  14.1 us (5%)
  local copies, waits for them, and re-layouts  11.1 us (4%)
  other arithmetic  6.31 us (2%)
    pallas_call x1, Pallas kernels, exchange(): pl.pallas_call(functools.partial(exchange_kernel, sizes), out_shape=(jax....  221 us
    pallas_call x1, Pallas kernels, leaf(): pl.pallas_call(leaf_kernel, out_shape=jax.ShapeDtypeStruct((col_count //...  15.7 us
    pallas_call x1, Pallas kernels, gather(): pl.pallas_call(functools.partial(gather_kernel, sizes), out_shape=jax.Sha...  13.2 us
    unnamed x11, local copies, waits for them, and re-layouts  11.1 us
    pallas_call x1, Pallas kernels, final(): pl.pallas_call(functools.partial(final_kernel, scale), out_shape=(shape,...  10.8 us
    dot_general x1, matrix products, per_device(): solved = jnp.dot(inverse[:, :col_count], panel, precision=PRECISE)  6.5 us

profile of v2, /device:TPU:0, one launch (start us, length us, event | category | flops | bytes accessed | tf_op | source)
XLA Modules:
  0.0 292.8 jit_solution(12162776854137213784)
XLA Ops:
  0.6 0.9 convert_reduce_fusion.1
  1.5 0.7 multiply_add_fusion
  2.2 0.7 convert_reduce_fusion
  3.0 0.8 convert_element_type.22
  3.8 2.5 multiply_bitcast_fusion
  6.3 0.7 copy.12
  7.1 3.6 %fusion.2 = f32[64,128,128]{2,1,0:T(8,128)S(1)} fusion(f32[64,128,128]{2,1,0:T(8,128)S(1)} %bitcast.23), kind=kOutput, calls=%fused_computation.6 | convolution fusion | flops 1611022336 | bytes 8388608 | tf_op jit(solution)/shard_map/cab,bk->cak/dot_general | solution.py:434
  10.7 4.0 %convolution_multiply_fusion.1 = f32[128,64,128]{2,0,1:T(8,128)S(1)} fusion(f32[64,128,128]{2,1,0:T(8,128)S(1)} %fusion.2), kind=kOutput, calls=%fused_computation.3 | convolution fusion | flops 1612070912 | bytes 8388608 | tf_op jit(solution)/shard_map/cab,ak->ckb/dot_general | solution.py:435
  14.7 4.4 %copy.15 = f32[8,8,128,128]{3,1,2,0:T(8,128)} copy(f32[8,8,128,128]{3,2,1,0:T(8,128)S(1)} %bitcast.24) | data formatting | bytes 8388608
  19.1 220.9 %exchange.1 = (f32[64,16384]{1,0:T(8,128)}, f32[32,64,128]{2,1,0:T(8,128)S(1)}) custom-call(s32[32]{0:T(128)S(1)} %get-tuple-element.21.from_ref, f32[32]{0:T(128)S(1)} %convert_element_type.20.used_ref, f32[64,16384]{1,0:T(8,128)} %bitcast.22), custom_call_target="tpu_custom_call" | custom-call | tf_op jit(solution)/shard_map/exchange/pallas_call | solution.py:224
  240.0 15.7 %leaf.1.leaf_ref = f32[32,128]{1,0:T(8,128)S(1)} custom-call(f32[32,64,128]{2,1,0:T(8,128)S(1)} %get-tuple-element.9.sketch_ref), custom_call_target="tpu_custom_call" | custom-call | tf_op jit(solution)/shard_map/leaf/pallas_call | solution.py:299
  255.7 0.0 copy-start.1
  255.7 0.6 copy-done.1
  256.3 13.2 %gather.1.all_ref = f32[32,32,128]{2,1,0:T(8,128)} custom-call(f32[32,128]{1,0:T(8,128)} %copy-done.1), custom_call_target="tpu_custom_call" | custom-call | tf_op jit(solution)/shard_map/gather/pallas_call | solution.py:353
  269.5 0.0 copy-start
  269.5 1.0 copy-done
  270.5 10.8 %final.1 = (f32[64,128]{1,0:T(8,128)S(1)}, f32[64,128]{1,0:T(8,128)S(1)}) custom-call(f32[32,32,128]{2,1,0:T(8,128)S(1)} %copy-done), custom_call_target="tpu_custom_call" | custom-call | tf_op jit(solution)/shard_map/final/pallas_call | solution.py:405
  281.4 0.7 copy.11
  282.1 0.0 copy-start.2
  282.1 6.5 %fusion = f32[16384]{0:T(1024)S(1)} fusion(f32[64,16384]{1,0:T(8,128)} %param.4, f32[64,128]{1,0:T(8,128)S(1)} %get-tuple-element.11), kind=kOutput, calls=%fused_computation.4 | convolution fusion | flops 807387136 | bytes 4292608 | tf_op jit(solution)/shard_map/dot_general | solution.py:442
  288.6 0.6 broadcast_multiply_fusion
  289.2 1.6 copy.10
  290.8 0.0 copy-done.2
  290.8 2.0 copy.17
  (2 shorter events, 0.0 us)
Async XLA Ops:
  255.7 0.6 copy-start.1
  269.5 1.0 copy-start
  282.1 8.7 %copy-start.2 = (f32[64,16384]{1,0:T(8,128)S(1)}, f32[64,16384]{1,0:T(8,128)}, u32[]{:S(2)}) copy-start(f32[64,16384]{1,0:T(8,128)} %get-tuple-element.26) | copy-start | bytes 12582916

commit v3 on v2

--- a/solution.py
+++ b/solution.py
@@ -107,8 +107,9 @@
 
 
 def exchange_kernel(sizes, from_ref, used_ref, x_ref, mixed_ref, sketch_ref, land, staged,
-                    keep, send_sem, recv_sem, out_sem, in_sem):
-    col_count, row_count = x_ref.shape
+                    keep, local, send_sem, recv_sem, out_sem, in_sem):
+    block_count, col_count, _ = x_ref.shape
+    row_count = block_count * BLOCK
     chunks = col_count // SUB
     low_count = sizes["ry"]
     bits = bits_of(sizes)
@@ -141,7 +142,7 @@
 
     def source(unit, step):
         if step == 0:
-            return x_ref.at[piece(unit)]
+            return local.at[piece(unit)]
         return land.at[(bits.index(orders[unit][step - 1]),) + piece(unit)]
 
     flight, arrivals, done = {}, [], [0] * chunks
@@ -149,6 +150,17 @@
         bit = orders[unit][step]
         where = bits.index(bit)
         own, other = source(unit, step), land.at[(where,) + piece(unit)]
+        if kind == "start" and step == 0:
+            start = unit % PARTS * part // BLOCK
+
+            def lay(group, carry, unit=unit, start=start):
+                for at in range(STRIP // BLOCK):
+                    block = start + group * (STRIP // BLOCK) + at
+                    lanes = pl.ds(pl.multiple_of(block * BLOCK, BLOCK), BLOCK)
+                    local[columns(unit // PARTS), lanes] = x_ref[block, columns(unit // PARTS), :]
+                return carry
+
+            lax.fori_loop(0, part // STRIP, lay, 0)
         if kind == "start":
             copy = pltpu.make_async_remote_copy(
                 src_ref=own,
@@ -215,7 +227,8 @@
 
 
 def exchange(sizes, x, from_block, used):
-    col_count, row_count = x.shape
+    block_count, col_count, _ = x.shape
+    row_count = block_count * BLOCK
     chunks = col_count // SUB
     slots = sizes["ry"] * CAP
     bit_count = len(bits_of(sizes))
@@ -233,13 +246,14 @@
             pltpu.VMEM((bit_count, col_count, row_count), jnp.float32),
             pltpu.VMEM((slots, col_count, BLOCK), jnp.float32),
             pltpu.VMEM((chunks, row_count // BLOCK, SUB, BLOCK), jnp.float32),
+            pltpu.VMEM((col_count, row_count), jnp.float32),
             pltpu.SemaphoreType.DMA((bit_count, chunks * PARTS)),
             pltpu.SemaphoreType.DMA((bit_count, chunks * PARTS)),
             pltpu.SemaphoreType.DMA((sizes["ry"] - 1, chunks)),
             pltpu.SemaphoreType.DMA((sizes["ry"] - 1, chunks)),
         ],
         compiler_params=pltpu.CompilerParams(
-            collective_id=0, has_side_effects=True, vmem_limit_bytes=50 * 2**20
+            collective_id=0, has_side_effects=True, vmem_limit_bytes=56 * 2**20
         ),
         name="exchange",
     )(from_block, used, x)
@@ -432,8 +446,8 @@
     signed = panel * signs.astype(jnp.float32)[None, :]
     blocked = signed.reshape(col_count, block_rows, LANES)
     blocked = jnp.einsum("cab,bk->cak", blocked, hadamard(LANES), precision=PRECISE)
-    blocked = jnp.einsum("cab,ak->ckb", blocked, hadamard(block_rows), precision=PRECISE)
-    local = blocked.reshape(col_count, row_count) * (1.0 / math.sqrt(row_count * device_count))
+    blocked = jnp.einsum("cab,ak->kcb", blocked, hadamard(block_rows), precision=PRECISE)
+    local = blocked * (1.0 / math.sqrt(row_count * device_count))
     mixed, sketch = exchange(sizes, local, from_block, used)
     received = jnp.transpose(sketch, (1, 0, 2))
     all_leaves = gather(sizes, leaf(sketch))

time: 293 us -> 296 us (1.010)
  other arithmetic: 6.31 us -> 12 us
  local copies, waits for them, and re-layouts: 11.1 us -> 7.92 us
    mul x0 -> x1, other arithmetic: none -> 4.71 us  [per_device(): local = blocked * (1.0 / math.sqrt(row_count * device_count))]
    unnamed x11 -> x14, local copies, waits for them, and re-layouts: 11.1 us -> 7.91 us
where the time goes in v3:
time: 296 us
  Pallas kernels  261 us (88%)
  matrix products  14 us (5%)
  other arithmetic  12 us (4%)
  local copies, waits for them, and re-layouts  7.92 us (3%)
    pallas_call x1, Pallas kernels, exchange(): pl.pallas_call(functools.partial(exchange_kernel, sizes), out_shape=(jax....  222 us
    pallas_call x1, Pallas kernels, leaf(): pl.pallas_call(leaf_kernel, out_shape=jax.ShapeDtypeStruct((col_count //...  15.7 us
    pallas_call x1, Pallas kernels, gather(): pl.pallas_call(functools.partial(gather_kernel, sizes), out_shape=jax.Sha...  13.2 us
    pallas_call x1, Pallas kernels, final(): pl.pallas_call(functools.partial(final_kernel, scale), out_shape=(shape,...  10.8 us
    unnamed x14, local copies, waits for them, and re-layouts  7.91 us
    dot_general x1, matrix products, per_device(): solved = jnp.dot(inverse[:, :col_count], panel, precision=PRECISE)  6.5 us

profile of v3, /device:TPU:0, one launch (start us, length us, event | category | flops | bytes accessed | tf_op | source)
XLA Modules:
  0.0 295.9 jit_solution(12885911961979516736)
XLA Ops:
  0.6 0.9 convert_reduce_fusion.1
  1.5 0.7 multiply_add_fusion
  2.2 1.3 convert_reduce_fusion
  3.5 0.5 convert_element_type.20.used_ref
  4.0 0.8 convert_element_type.22
  4.8 2.5 multiply_bitcast_fusion
  7.3 0.7 copy.14
  8.1 3.6 %fusion.3 = f32[64,128,128]{2,1,0:T(8,128)S(1)} fusion(f32[64,128,128]{2,1,0:T(8,128)S(1)} %bitcast.17), kind=kOutput, calls=%fused_computation.6 | convolution fusion | flops 1611022336 | bytes 8388608 | tf_op jit(solution)/shard_map/cab,bk->cak/dot_general | solution.py:448
  11.7 3.8 %fusion.1 = f32[128,64,128]{2,0,1:T(8,128)S(1)} fusion(f32[64,128,128]{2,1,0:T(8,128)S(1)} %fusion.3), kind=kOutput, calls=%fused_computation.4 | convolution fusion | flops 1611022336 | bytes 8388608 | tf_op jit(solution)/shard_map/cab,ak->kcb/dot_general | solution.py:449
  15.6 4.7 %copy_multiply_fusion.x_ref = f32[128,64,128]{2,1,0:T(8,128)} fusion(f32[128,64,128]{2,0,1:T(8,128)S(1)} %fusion.1), kind=kLoop, calls=%fused_computation.1 | loop fusion | flops 1048576 | bytes 8388608 | tf_op jit(solution)/shard_map/mul | solution.py:450
  20.3 221.6 %exchange.1 = (f32[64,16384]{1,0:T(8,128)}, f32[32,64,128]{2,1,0:T(8,128)}) custom-call(s32[32]{0:T(128)} %get-tuple-element.21.from_ref, f32[32]{0:T(128)} %convert_element_type.20.used_ref, f32[128,64,128]{2,1,0:T(8,128)} %copy_multiply_fusion.x_ref), custom_call_target="tpu_custom_call" | custom-call | tf_op jit(solution)/shard_map/exchange/pallas_call | solution.py:237
  241.9 0.0 copy-start
  241.9 1.2 copy-done
  243.1 0.0 copy-start.1
  243.1 15.7 %leaf.1.leaf_ref = f32[32,128]{1,0:T(8,128)S(1)} custom-call(f32[32,64,128]{2,1,0:T(8,128)S(1)} %copy-done), custom_call_target="tpu_custom_call" | custom-call | tf_op jit(solution)/shard_map/leaf/pallas_call | solution.py:313
  258.8 0.0 copy-start.3
  258.8 0.6 copy-done.3
  259.4 13.2 %gather.1.all_ref = f32[32,32,128]{2,1,0:T(8,128)} custom-call(f32[32,128]{1,0:T(8,128)} %copy-done.3), custom_call_target="tpu_custom_call" | custom-call | tf_op jit(solution)/shard_map/gather/pallas_call | solution.py:367
  272.6 0.0 copy-start.2
  272.6 1.0 copy-done.2
  273.6 10.8 %final.1 = (f32[64,128]{1,0:T(8,128)S(1)}, f32[64,128]{1,0:T(8,128)S(1)}) custom-call(f32[32,32,128]{2,1,0:T(8,128)S(1)} %copy-done.2), custom_call_target="tpu_custom_call" | custom-call | tf_op jit(solution)/shard_map/final/pallas_call | solution.py:419
  284.5 0.7 copy.13
  285.2 0.0 copy-start.4
  285.2 6.5 %fusion = f32[16384]{0:T(1024)S(1)} fusion(f32[64,16384]{1,0:T(8,128)} %param.4, f32[64,128]{1,0:T(8,128)S(1)} %get-tuple-element.11), kind=kOutput, calls=%fused_computation.3 | convolution fusion | flops 807387136 | bytes 4292608 | tf_op jit(solution)/shard_map/dot_general | solution.py:456
  291.7 0.6 broadcast_multiply_fusion
  292.3 0.0 copy-done.1
  292.3 1.6 copy.12
  293.9 0.0 copy-done.4
  293.9 2.0 copy.17
  (1 shorter events, 0.0 us)
Async XLA Ops:
  241.9 1.2 copy-start
  243.1 49.2 %copy-start.1 = (f32[32,64,128]{2,1,0:T(8,128)S(1)}, f32[32,64,128]{2,1,0:T(8,128)}, u32[]{:S(2)}) copy-start(f32[32,64,128]{2,1,0:T(8,128)} %get-tuple-element.9.sketch_ref) | copy-start | bytes 3145732
  258.8 0.6 copy-start.3
  272.6 1.0 copy-start.2
  285.2 8.7 %copy-start.4 = (f32[64,16384]{1,0:T(8,128)S(1)}, f32[64,16384]{1,0:T(8,128)}, u32[]{:S(2)}) copy-start(f32[64,16384]{1,0:T(8,128)} %get-tuple-element.26) | copy-start | bytes 12582916
